TPU v7x, 32 devices: a whole 2x2x4 slice. The times are simulated.
32 devices in a mesh: seg: 8 (over z, y), blk: 4 (over x, core).
Axes of the slice: x: 2, y: 2, z: 4, core: 2. Of those that a mesh axis runs over, the one named last changes fastest.
Arguments:
- queries: float32 [4096, 1024], P(('seg', 'blk')), may hold values from -5 to 5
- keys: float32 [4096, 256], P(('seg', 'blk')), may hold values from -5 to 5
- values: float32 [4096, 256], P(('seg', 'blk')), may hold values from -6 to 6
- gate_logit: float32 [8], replicated, may hold values from -3 to 3
- memory_gain: float32 [1024], replicated, may hold values from 0.5 to 2
Outputs:
- mixed: float32 [4096, 1024], P(('seg', 'blk'))
All inputs are finite; a program needn't handle non-finite values.
Results may differ from a plain program's by a relative error of at most 0.0003.
Values sent between devices are 32-bit elements; how exact they have to be, the bound alone decides.
No kernel may reach another device: no remote copies, remote signals or barrier semaphores. Data moves between devices by JAX's collectives and lax.ppermute only.
A program may use at most 64 MiB of HBM per device.

v0:
```python
import jax
import jax.numpy as jnp
from jax import lax
from jax.sharding import PartitionSpec as P

QH = 8
KVH = 2
GROUP = 4
HD = 128
HIGH = lax.Precision.HIGHEST


def prefix_2(part, axis, combine, identity):
    place = lax.axis_index(axis)
    gathered = lax.all_gather(part, axis)
    state = jnp.zeros_like(part) + jnp.asarray(identity, part.dtype)

    def one(lap, state):
        return combine(state, lax.dynamic_index_in_dim(gathered, lap, 0, False))

    return lax.fori_loop(0, place, one, state)


def sigma_map(x):
    return jnp.where(x > 0, x + 1.0, jnp.exp(jnp.minimum(x, 0.0)))


def add_terms(earlier, later):
    return earlier + later


def on_device(queries, keys, values, gate_logit, memory_gain):
    rows = queries.shape[0]
    index = lax.axis_index("blk")
    q_heads = queries.reshape(rows, KVH, GROUP, HD)
    qpos = index * rows + jnp.arange(rows, dtype=jnp.int32)
    scale = 1.0 / jnp.sqrt(jnp.float32(HD))

    def update(carry, pieces):
        top, total, accum = carry
        k_piece, v_piece = pieces
        count = k_piece.shape[0]
        k_h = k_piece.reshape(count, KVH, HD)
        v_h = v_piece.reshape(count, KVH, HD)
        scores = jnp.einsum("rkgd,nkd->kgrn", q_heads, k_h, precision=HIGH) * scale
        kpos = jnp.arange(count, dtype=jnp.int32)
        allowed = (kpos[None, :] <= qpos[:, None])[None, None]
        row_top = jnp.max(jnp.where(allowed, scores, -1e30), axis=-1)
        new_top = jnp.maximum(top, row_top)
        weights = jnp.where(allowed, jnp.exp(scores - new_top[..., None]), 0.0)
        total = jnp.sum(weights, axis=-1)
        accum = jnp.einsum("kgrn,nkd->kgrd", weights, v_h, precision=HIGH)
        return (new_top, total, accum)

    start_state = (
        jnp.full((KVH, GROUP, rows), -1e30, jnp.float32),
        jnp.zeros((KVH, GROUP, rows), jnp.float32),
        jnp.zeros((KVH, GROUP, rows, HD), jnp.float32),
    )
    pieces = (
        lax.all_gather(keys, "blk", axis=0, tiled=True),
        lax.all_gather(values, "blk", axis=0, tiled=True),
    )
    top, total, accum = lax.cond(
        jnp.int32(0) <= qpos[rows - 1], lambda c: update(c, pieces), lambda c: c, start_state
    )
    attention = accum / total[..., None]
    sig_keys = sigma_map(keys.reshape(rows, KVH, HD))
    partial_value = jnp.einsum(
        "rkd,rke->kde", sig_keys, values.reshape(rows, KVH, HD), precision=HIGH
    ).reshape(KVH * HD, HD)
    shard = lax.psum_scatter(partial_value, "blk", scatter_dimension=0, tiled=True)
    prefix = prefix_2(shard, "seg", add_terms, jnp.zeros_like(shard))
    memory = lax.all_gather(prefix, "blk", axis=0, tiled=True)
    retrieval = jnp.einsum(
        "rkgd,kde->kgre", sigma_map(q_heads), memory.reshape(KVH, HD, HD), precision=HIGH
    )
    rms = jnp.sqrt(jnp.mean(retrieval * retrieval, axis=-1, keepdims=True) + 1e-06)
    normed = retrieval / rms * memory_gain.reshape(KVH, GROUP, 1, HD)
    gate = jax.nn.sigmoid(gate_logit).reshape(KVH, GROUP, 1, 1)
    mixed = gate * normed + (1.0 - gate) * attention
    return jnp.transpose(mixed, (2, 0, 1, 3)).reshape(rows, QH * HD)


def solution(mesh):
    return jax.shard_map(
        on_device,
        mesh=mesh,
        in_specs=(
            P(("seg", "blk"), None),
            P(("seg", "blk"), None),
            P(("seg", "blk"), None),
            P(),
            P(),
        ),
        out_specs=P(("seg", "blk"), None),
        check_vma=False,
    )
```

profile of v0, /device:TPU:0, one launch (start us, length us, event | category | flops | bytes accessed | tf_op | source)
XLA Modules:
  0.0 82.2 jit_solution(3702383600021202158)
XLA Ops:
  6.5 0.0 copy-start.2
  6.5 0.0 copy-start
  6.5 0.0 reduce-scatter.2.cloned.1.call-start
  6.5 1.0 %exponential_select_fusion = f32[128,256]{1,0:T(8,128)S(1)} fusion(f32[128,256]{1,0:T(8,128)} %param.10), kind=kLoop, calls=%fused_computation.32 | loop fusion | flops 131072 | bytes 262144 | tf_op jit(solution)/shard_map/jit(_where)/select_n | solution.py:25
  7.5 0.1 copy.34
  7.6 1.8 %fusion.22 = f32[2,128,128]{2,1,0:T(8,128)} fusion(f32[128,2,128]{0,2,1:T(8,128)S(1)} %bitcast.51, f32[128,256]{1,0:T(8,128)} %param.11), kind=kOutput, calls=%fused_computation.29 | convolution fusion | flops 50331648 | bytes 393216 | tf_op jit(solution)/shard_map/rkd,rke->kde/dot_general | solution.py:69
  9.5 0.0 reduce-scatter.2.cloned.1.call-update
  9.5 8.8 %all_gather.18 = f32[512,256]{1,0:T(8,128)S(1)} all-gather(f32[128,256]{1,0:T(8,128)} %param.10), channel_id=1, replica_groups=mesh['seg'=8,'blk'=4] {'blk'}, dimensions={0}, use_global_device_ids=true | all-gather | bytes 655360 | tf_op jit(solution)/shard_map/all_gather | solution.py:61
  18.3 8.8 %all_gather.19 = f32[512,256]{1,0:T(8,128)} all-gather(f32[128,256]{1,0:T(8,128)} %param.11), channel_id=1, replica_groups=mesh['seg'=8,'blk'=4] {'blk'}, dimensions={0}, use_global_device_ids=true | all-gather | bytes 655360 | tf_op jit(solution)/shard_map/all_gather | solution.py:62
  27.2 0.0 copy-done.2
  27.2 0.0 copy-done
  27.2 0.2 copy.18
  27.4 0.6 slice.3
  28.6 0.1 mul.40
  28.7 6.7 %conditional.1 = (f32[2,4,128]{2,1,0:T(4,128)S(1)}, f32[2,4,128,128]{2,3,1,0:T(8,128)}) conditional(s32[]{:T(128)} %bitcast.12, () %tuple.18, (s32[128]{0:T(128)S(1)}, f32[512,256]{1,0:T(8,128)S(1)}, f32[128,2,4,128]{0,3,2,1:T(8,128)S(1)}, f32[512,256]{1,0:T(8,128)}) %tuple.40), branch_computations={%region_4.5_spmd, %region_5.8_spmd} | conditional | flops 1615920128 | bytes 10773008 | solution.py:64
  28.8 0.3 reshape.68
  29.0 2.0 %fusion = (f32[2,4,128]{2,1,0:T(4,128)S(1)}, f32[2,512,128,4]{2,1,3,0:T(8,128)S(1)}) fusion(pred[128,512]{0,1:T(8,128)(4,1)S(1)} %iota_compare_fusion, f32[128,2,4,128]{0,3,2,1:T(8,128)S(1)} %get-tuple-element.47, f32[512,2,128,1]{2,1,0,3:T(2,128)S(1)} %bitcast.46), kind=kOutput, calls=%fused_computation.3 | convolution fusion | flops 806878208 | bytes 3215360 | tf_op jit(solution)/shard_map/cond/branch_1_fun/rkgd,nkd->kgrn/dot_general | solution.py:45
  31.0 1.3 %reshape.69 = f32[512,2,128]{2,1,0:T(2,128)S(1)} reshape(f32[512,256]{1,0:T(8,128)} %get-tuple-element.38) | data formatting | bytes 1048576 | tf_op jit(solution)/shard_map/cond/branch_1_fun/reshape | solution.py:44
  32.3 2.6 %fusion.3 = f32[2,4,128,128]{2,3,1,0:T(8,128)} fusion(f32[2,512,128,4]{2,1,3,0:T(8,128)S(1)} %get-tuple-element.59, f32[2,4,128]{2,1,0:T(4,128)S(1)} %broadcast_maximum_fusion, pred[128,512]{0,1:T(8,128)(4,1)S(1)} %iota_compare_fusion, f32[512,2,128,1]{2,1,0,3:T(2,128)S(1)} %bitcast.52), kind=kOutput, calls=%fused_computation.6 | convolution fusion | flops 806879232 | bytes 3215360 | tf_op jit(solution)/shard_map/cond | solution.py:64
  34.9 0.4 fusion.5
  35.4 0.0 copy-start.1
  35.4 0.0 reduce-scatter.2.cloned.1.call-done
  35.4 31.5 %all-gather = f32[512,128]{1,0:T(8,128)S(1)} all-gather(f32[64,128]{1,0:T(8,128)} %reduce-scatter.2.cloned.1.call-done), channel_id=2, replica_groups=mesh['seg'=8,'blk'=4] {'seg'}, dimensions={0}, use_global_device_ids=true | all-gather | bytes 294912 | tf_op jit(solution)/shard_map/all_gather | solution.py:15
  66.9 5.4 %all_gather.17 = f32[256,128]{1,0:T(8,128)S(1)} all-gather(f32[64,128]{1,0:T(8,128)S(1)} %get-tuple-element.42), channel_id=1, replica_groups=mesh['seg'=8,'blk'=4] {'blk'}, dimensions={0}, use_global_device_ids=true | all-gather | bytes 163840 | tf_op jit(solution)/shard_map/all_gather | solution.py:74
  72.3 0.7 multiply_reduce_fusion
  73.0 0.0 copy-done.1
  73.0 1.3 %multiply_add_fusion = f32[2,4,128,128]{2,3,1,0:T(8,128)S(1)} fusion(f32[2,4,128,128]{2,3,1,0:T(8,128)} %get-tuple-element.49, f32[2,4,128,128]{2,3,1,0:T(8,128)S(1)} %get-tuple-element.61, f32[2,4,128]{2,1,0:T(4,128)S(1)} %get-tuple-element.44, f32[2,4]{1,0:T(2,128)S(1)} %broadcast_subtract_fusion, f32[2,4,128]{2,1,0:T(4,128)S(1)} %bitcast.53, ...), kind=kLoop, calls=%fused_computation.20 | loop fusion | flops 786432 | bytes 1585216 | tf_op jit(solution)/shard_map/add | solution.py:81
  74.3 1.0 %copy.23 = f32[128,1024]{1,0:T(8,128)} copy(f32[128,1024]{0,1:T(8,128)S(1)} %bitcast.47) | data formatting | bytes 1048576 | tf_op jit(solution)/shard_map/reshape | solution.py:82
  (8 shorter events, 0.1 us)
Async XLA Ops:
  6.5 20.6 %copy-start.2 = (f32[8]{0:T(128)S(1)}, f32[8]{0:T(128)}, u32[]{:S(2)}) copy-start(f32[8]{0:T(128)} %param.12) | copy-start | bytes 100
  6.5 20.6 %copy-start = (f32[128,1024]{1,0:T(8,128)S(1)}, f32[128,1024]{1,0:T(8,128)}, u32[]{:S(2)}) copy-start(f32[128,1024]{1,0:T(8,128)} %param.9) | copy-start | bytes 1572868
  6.5 28.9 %reduce-scatter.2.cloned.1.call-start = ((), (), s32[]{:S(2)}) async-start(), calls=%async_computation.1 | async-start | bytes 163840 | tf_op jit(solution)/shard_map/reduce_scatter | solution.py:72
  35.4 37.7 %copy-start.1 = (f32[1024]{0:T(1024)S(1)}, f32[1024]{0:T(1024)}, u32[]{:S(2)}) copy-start(f32[1024]{0:T(1024)} %param.13) | copy-start | bytes 12292
Sparse Core Ops, SparseCore 0:
  9.8 22.2 reduce-scatter.1
where the time goes:
time: 82.5 us; the launch traced here: 82.2 us
  blocking collectives  54.6 us (66%)
  between operations  14.1 us (17%)
  matrix products  7.09 us (9%)
  local copies, waits for them, and re-layouts  3.53 us (4%)
  other arithmetic  2.79 us (3%)
    all_gather x1, blocking collectives, prefix_2(): gathered = lax.all_gather(part, axis)  31.5 us
    all_gather x1, blocking collectives, on_device(): lax.all_gather(values, 'blk', axis=0, tiled=True)  8.84 us
    all_gather x1, blocking collectives, on_device(): lax.all_gather(keys, 'blk', axis=0, tiled=True)  8.83 us
    all_gather x1, blocking collectives, on_device(): memory = lax.all_gather(prefix, 'blk', axis=0, tiled=True)  5.42 us
    cond x1, matrix products, on_device(): lax.cond(jnp.int32(0) <= qpos[rows - 1], lambda c: update(c, pieces), lam...  2.61 us
    dot_general x1, matrix products, update(): scores = jnp.einsum('rkgd,nkd->kgrn', q_heads, k_h, precision=HIGH) * scale  1.96 us
    dot_general x1, matrix products, on_device(): jnp.einsum('rkd,rke->kde', sig_keys, values.reshape(rows, KVH, HD), preci...  1.83 us
  transfers between devices with their start and end apart: 1, of which 0 were waited for; matrix products, arithmetic and copies ran while one was open for 9% of the time, Pallas kernels for 0%

commit v1 on v0

--- a/solution.py
+++ b/solution.py
@@ -71,7 +71,12 @@
     ).reshape(KVH * HD, HD)
     shard = lax.psum_scatter(partial_value, "blk", scatter_dimension=0, tiled=True)
     prefix = prefix_2(shard, "seg", add_terms, jnp.zeros_like(shard))
-    memory = lax.all_gather(prefix, "blk", axis=0, tiled=True)
+    ring = [prefix]
+    for hop in range(3):
+        ring.append(lax.ppermute(ring[-1], "blk", [(dev, (dev + 1) % 4) for dev in range(4)]))
+    memory = jnp.roll(
+        jnp.concatenate(ring[::-1], axis=0), (lax.axis_index("blk") + 1) * ring[0].shape[0], axis=0
+    )
     retrieval = jnp.einsum(
         "rkgd,kde->kgre", sigma_map(q_heads), memory.reshape(KVH, HD, HD), precision=HIGH
     )

time: 82.5 us -> 99.1 us (1.20)
  waiting for transfers between devices: 0.04 us -> 21.9 us
  blocking collectives: 54.6 us -> 46.3 us
  matrix products: 7.09 us -> 8.13 us
    reduce_scatter x1, waiting for transfers between devices: 0.02 us -> 21.8 us  [on_device(): lax.psum_scatter(partial_value, 'blk', scatter_dimension=0, tiled=True)]
    all_gather x1 -> x0, blocking collectives: 5.42 us -> none  [on_device(): memory = lax.all_gather(prefix, 'blk', axis=0, tiled=True)]
    all_gather x1, blocking collectives: 8.83 us -> 7.59 us  [on_device(): lax.all_gather(keys, 'blk', axis=0, tiled=True)]
    all_gather x1, blocking collectives: 8.84 us -> 7.75 us  [on_device(): lax.all_gather(values, 'blk', axis=0, tiled=True)]
    cond x1, matrix products: 2.61 us -> 3.64 us  [on_device(): lax.cond(jnp.int32(0) <= qpos[rows - 1], lambda c: update(c, pieces), lam...]
  transfers between devices with their start and end apart: 1 -> 4, of which waited for: 0 -> 1; matrix products, arithmetic and copies ran while one was open for 9% -> 9% of each run, Pallas kernels for 0% -> 0%
where the time goes in v1:
time: 99.1 us; the launch traced here: 98.7 us
  blocking collectives  46.3 us (47%)
  waiting for transfers between devices  21.9 us (22%)
  between operations  14.2 us (14%)
  matrix products  8.13 us (8%)
  local copies, waits for them, and re-layouts  3.92 us (4%)
  other arithmetic  3.46 us (3%)
    all_gather x1, blocking collectives, prefix_2(): gathered = lax.all_gather(part, axis)  31 us
    reduce_scatter x1, waiting for transfers between devices, on_device(): lax.psum_scatter(partial_value, 'blk', scatter_dimension=0, tiled=True)  21.8 us
    all_gather x1, blocking collectives, on_device(): lax.all_gather(values, 'blk', axis=0, tiled=True)  7.75 us
    all_gather x1, blocking collectives, on_device(): lax.all_gather(keys, 'blk', axis=0, tiled=True)  7.59 us
    cond x1, matrix products, on_device(): lax.cond(jnp.int32(0) <= qpos[rows - 1], lambda c: update(c, pieces), lam...  3.64 us
  transfers between devices with their start and end apart: 4, of which 1 were waited for; matrix products, arithmetic and copies ran while one was open for 9% of the time, Pallas kernels for 0%

profile of v1, /device:TPU:0, one launch (start us, length us, event | category | flops | bytes accessed | tf_op | source)
XLA Modules:
  0.0 98.7 jit_solution(5421183968647977960)
XLA Ops:
  6.5 0.0 reduce-scatter.2.cloned.1.call-start
  6.5 1.0 %exponential_select_fusion = f32[128,256]{1,0:T(8,128)S(1)} fusion(f32[128,256]{1,0:T(8,128)} %param.10), kind=kLoop, calls=%fused_computation.32 | loop fusion | flops 131072 | bytes 262144 | tf_op jit(solution)/shard_map/jit(_where)/select_n | solution.py:25
  7.6 0.1 copy.34
  7.7 1.8 %fusion.22 = f32[2,128,128]{2,1,0:T(8,128)} fusion(f32[128,2,128]{0,2,1:T(8,128)S(1)} %bitcast.51, f32[128,256]{1,0:T(8,128)} %param.11), kind=kOutput, calls=%fused_computation.29 | convolution fusion | flops 50331648 | bytes 393216 | tf_op jit(solution)/shard_map/rkd,rke->kde/dot_general | solution.py:69
  9.5 0.0 reduce-scatter.2.cloned.1.call-update
  9.5 0.7 add_divide_fusion
  10.2 0.1 mul.43
  10.3 21.8 %reduce-scatter.2.cloned.1.call-done = f32[64,128]{1,0:T(8,128)} async-done(((f32[256,128]{1,0:T(8,128)}), f32[64,128]{1,0:T(8,128)}) %reduce-scatter.2.cloned.1.call-update) | async-done | bytes 32784 | tf_op jit(solution)/shard_map/reduce_scatter | solution.py:72
  32.1 31.0 %all-gather = f32[512,128]{1,0:T(8,128)S(1)} all-gather(f32[64,128]{1,0:T(8,128)} %reduce-scatter.2.cloned.1.call-done), channel_id=2, replica_groups=mesh['seg'=8,'blk'=4] {'seg'}, dimensions={0}, use_global_device_ids=true | all-gather | bytes 294912 | tf_op jit(solution)/shard_map/all_gather | solution.py:15
  63.1 0.0 collective-permute-start
  63.1 0.0 copy-done.2
  63.2 7.6 %all_gather.14 = f32[512,256]{1,0:T(8,128)S(1)} all-gather(f32[128,256]{1,0:T(8,128)S(1)} %copy-done.2), channel_id=1, replica_groups=mesh['seg'=8,'blk'=4] {'blk'}, dimensions={0}, use_global_device_ids=true | all-gather | bytes 655360 | tf_op jit(solution)/shard_map/all_gather | solution.py:61
  70.7 0.0 collective-permute-done
  70.8 0.3 collective-permute-start.1
  71.1 0.0 copy-done.1
  71.1 7.7 %all_gather.15 = f32[512,256]{1,0:T(8,128)} all-gather(f32[128,256]{1,0:T(8,128)S(1)} %copy-done.1), channel_id=1, replica_groups=mesh['seg'=8,'blk'=4] {'blk'}, dimensions={0}, use_global_device_ids=true | all-gather | bytes 655360 | tf_op jit(solution)/shard_map/all_gather | solution.py:62
  78.9 0.0 collective-permute-done.1
  78.9 0.3 collective-permute-start.2
  79.2 0.6 slice.3
  80.5 0.2 copy.18
  80.7 0.0 copy-start.4
  80.7 8.1 %conditional.1 = (f32[2,4,128]{2,1,0:T(4,128)S(1)}, f32[2,4,128,128]{2,3,1,0:T(8,128)}) conditional(s32[]{:T(128)} %bitcast.12, () %tuple.18, (s32[128]{0:T(128)S(1)}, f32[512,256]{1,0:T(8,128)S(1)}, f32[128,2,4,128]{0,3,2,1:T(8,128)S(1)}, f32[512,256]{1,0:T(8,128)}) %tuple.40), branch_computations={%region_4.5_spmd, %region_5.8_spmd} | conditional | flops 1615920128 | bytes 12870188 | solution.py:64
  80.8 0.3 reshape.68
  81.0 2.0 %fusion = (f32[2,4,128]{2,1,0:T(4,128)S(1)}, f32[2,512,128,4]{2,1,3,0:T(8,128)S(1)}) fusion(pred[128,512]{0,1:T(8,128)(4,1)S(1)} %iota_compare_fusion, f32[128,2,4,128]{0,3,2,1:T(8,128)S(1)} %get-tuple-element.47, f32[512,2,128,1]{2,1,0,3:T(2,128)S(1)} %bitcast.46), kind=kOutput, calls=%fused_computation.3 | convolution fusion | flops 806878208 | bytes 3215360 | tf_op jit(solution)/shard_map/cond/branch_1_fun/rkgd,nkd->kgrn/dot_general | solution.py:45
  83.0 0.4 fusion.5
  83.5 0.6 copy-done
  84.0 1.1 %reshape.69 = f32[512,2,128]{2,1,0:T(2,128)} reshape(f32[512,256]{1,0:T(8,128)S(1)} %copy-done) | data formatting | bytes 1048576 | tf_op jit(solution)/shard_map/cond/branch_1_fun/reshape | solution.py:44
  85.1 3.6 %fusion.3 = f32[2,4,128,128]{2,3,1,0:T(8,128)} fusion(f32[2,512,128,4]{2,1,3,0:T(8,128)S(1)} %get-tuple-element.59, f32[2,4,128]{2,1,0:T(4,128)S(1)} %broadcast_maximum_fusion, pred[128,512]{0,1:T(8,128)(4,1)S(1)} %iota_compare_fusion, f32[512,2,128,1]{2,1,0,3:T(2,128)} %bitcast.52), kind=kOutput, calls=%fused_computation.6 | convolution fusion | flops 806879232 | bytes 3215360 | tf_op jit(solution)/shard_map/cond | solution.py:64
  88.7 0.0 collective-permute-done.2
  88.9 0.7 multiply_reduce_fusion
  89.6 1.3 %multiply_add_fusion = f32[2,4,128,128]{2,3,1,0:T(8,128)S(1)} fusion(f32[2,4,128,128]{2,3,1,0:T(8,128)} %get-tuple-element.49, f32[2,4,128,128]{2,3,1,0:T(8,128)S(1)} %get-tuple-element.61, f32[2,4,128]{2,1,0:T(4,128)S(1)} %get-tuple-element.44, f32[2,4]{1,0:T(2,128)S(1)} %broadcast_subtract_fusion, f32[2,4,128]{2,1,0:T(4,128)S(1)} %bitcast.53, ...), kind=kLoop, calls=%fused_computation.20 | loop fusion | flops 786432 | bytes 1585216 | tf_op jit(solution)/shard_map/add | solution.py:86
  90.9 1.0 %copy.23 = f32[128,1024]{1,0:T(8,128)} copy(f32[128,1024]{0,1:T(8,128)S(1)} %bitcast.47) | data formatting | bytes 1048576 | tf_op jit(solution)/shard_map/reshape | solution.py:87
  (22 shorter events, 0.1 us)
Async XLA Ops:
  6.5 56.6 %copy-start.2 = (f32[128,256]{1,0:T(8,128)S(1)}, f32[128,256]{1,0:T(8,128)}, u32[]{:S(2)}) copy-start(f32[128,256]{1,0:T(8,128)} %param.10) | copy-start | bytes 393220
  6.5 64.6 %copy-start.1 = (f32[128,256]{1,0:T(8,128)S(1)}, f32[128,256]{1,0:T(8,128)}, u32[]{:S(2)}) copy-start(f32[128,256]{1,0:T(8,128)} %param.11) | copy-start | bytes 393220
  6.5 73.9 %copy-start.3 = (f32[128,1024]{1,0:T(8,128)S(1)}, f32[128,1024]{1,0:T(8,128)}, u32[]{:S(2)}) copy-start(f32[128,1024]{1,0:T(8,128)} %param.9) | copy-start | bytes 1572868
  6.5 25.6 %reduce-scatter.2.cloned.1.call-start = ((), (), s32[]{:S(2)}) async-start(), calls=%async_computation.1 | async-start | bytes 163840 | tf_op jit(solution)/shard_map/reduce_scatter | solution.py:72
  63.1 7.7 %collective-permute-start = (f32[64,128]{1,0:T(8,128)S(1)}, f32[64,128]{1,0:T(8,128)S(1)}, u32[]{:S(2)}, u32[]{:S(2)}) collective-permute-start(f32[64,128]{1,0:T(8,128)S(1)} %get-tuple-element.42), channel_id=1, source_target_pairs={{0,1},{1,2},{2,3},{3,0},{4,5},{5,6},{6,7},{7,4},{8,9},{9,10},{10,1... | collective-permute-start | bytes 98312 | tf_op jit(solution)/shard_map/ppermute | solution.py:76
  70.8 8.1 %collective-permute-start.1 = (f32[64,128]{1,0:T(8,128)S(1)}, f32[64,128]{1,0:T(8,128)S(1)}, u32[]{:S(2)}, u32[]{:S(2)}) collective-permute-start(f32[64,128]{1,0:T(8,128)S(1)} %collective-permute-done), channel_id=1, source_target_pairs={{0,1},{1,2},{2,3},{3,0},{4,5},{5,6},{6,7},{7,4},{8,9},{9,10},{10,1... | collective-permute-start | bytes 98312 | tf_op jit(solution)/shard_map/ppermute | solution.py:76
  78.9 9.9 %collective-permute-start.2 = (f32[64,128]{1,0:T(8,128)S(1)}, f32[64,128]{1,0:T(8,128)S(1)}, u32[]{:S(2)}, u32[]{:S(2)}) collective-permute-start(f32[64,128]{1,0:T(8,128)S(1)} %collective-permute-done.1), channel_id=1, source_target_pairs={{0,1},{1,2},{2,3},{3,0},{4,5},{5,6},{6,7},{7,4},{8,9},{9,10},{10,1... | collective-permute-start | bytes 98312 | tf_op jit(solution)/shard_map/ppermute | solution.py:76
  80.7 8.9 %copy-start.4 = (f32[1024]{0:T(1024)S(1)}, f32[1024]{0:T(1024)}, u32[]{:S(2)}) copy-start(f32[1024]{0:T(1024)} %param.13) | copy-start | bytes 12292
  83.0 1.0 %copy-start = (f32[512,256]{1,0:T(8,128)S(1)}, f32[512,256]{1,0:T(8,128)}, u32[]{:S(2)}) copy-start(f32[512,256]{1,0:T(8,128)} %get-tuple-element.38) | copy-start | bytes 1572868 | tf_op jit(solution)/shard_map/cond
Sparse Core Ops, SparseCore 0:
  9.8 22.2 reduce-scatter.1
